TPU v7x, 32 devices: a whole 2x2x4 slice. The times are simulated.
32 devices in a mesh: gx: 4 (over z), gy: 4 (over y, x), gz: 2 (over core).
Axes of the slice: x: 2, y: 2, z: 4, core: 2. Of those that a mesh axis runs over, the one named last changes fastest.
Arguments:
- populations: float32 [19, 16, 64, 256], P(None, 'gx', 'gy', 'gz'), may hold values from 0 to 0.2
- solid: int32 [16, 64, 256], P('gx', 'gy', 'gz'), may hold values 0 or 1
- rates: float32 [19], replicated, may hold values from 0.3 to 1.95
Outputs:
- evolved: float32 [19, 16, 64, 256], P(None, 'gx', 'gy', 'gz')
Inputs may be any that keep to these rules, and one draw needn't show every extreme that they name: solid holds only 0 and 1.
All inputs are finite; a program needn't handle non-finite values. No bound on the sum of `solid` on one device may be relied on, other than what follows from the above.
Results may differ from a plain program's by a relative error of at most 0.00011.
Values sent between devices are 32-bit elements; how exact they have to be, the bound alone decides.
A program may use at most 64 MiB of HBM per device.

v0:
```python
import jax
import jax.numpy as jnp
import numpy as np
from jax import lax
from jax.sharding import PartitionSpec as P

STEPS = 3


def from_behind(value, axis, steps):
    count = lax.axis_size(axis)
    pairs = [(source, (source + steps) % count) for source in range(count)]
    return lax.ppermute(value, axis, pairs)


def invert_table(matrix):
    dimension = matrix.shape[0]
    augmented = np.concatenate([matrix, np.eye(dimension)], axis=1)
    for column in range(dimension):
        pivot_row = column + int(np.argmax(np.abs(augmented[column:, column])))
        augmented[[column, pivot_row]] = augmented[[pivot_row, column]]
        augmented[column] = augmented[column] / augmented[column, column]
        for target_row in range(dimension):
            if target_row != column:
                augmented[target_row] = (
                    augmented[target_row] - augmented[target_row, column] * augmented[column]
                )
    return augmented[:, dimension:]


def tables():
    velocity = np.array(
        [
            [0, 0, 0],
            [1, 0, 0],
            [-1, 0, 0],
            [0, 1, 0],
            [0, -1, 0],
            [0, 0, 1],
            [0, 0, -1],
            [1, 1, 0],
            [-1, -1, 0],
            [1, -1, 0],
            [-1, 1, 0],
            [1, 0, 1],
            [-1, 0, -1],
            [1, 0, -1],
            [-1, 0, 1],
            [0, 1, 1],
            [0, -1, -1],
            [0, 1, -1],
            [0, -1, 1],
        ]
    )
    weights = np.array([1.0 / 3.0] + [1.0 / 18.0] * 6 + [1.0 / 36.0] * 12)
    exponents = [
        (0, 0, 0),
        (1, 0, 0),
        (0, 1, 0),
        (0, 0, 1),
        (2, 0, 0),
        (0, 2, 0),
        (0, 0, 2),
        (1, 1, 0),
        (1, 0, 1),
        (0, 1, 1),
        (2, 1, 0),
        (2, 0, 1),
        (1, 2, 0),
        (0, 2, 1),
        (1, 0, 2),
        (0, 1, 2),
        (2, 2, 0),
        (2, 0, 2),
        (0, 2, 2),
    ]
    moments = np.array(
        [
            [
                1.0
                * (
                    int(vel_row[0]) ** power[0]
                    * int(vel_row[1]) ** power[1]
                    * int(vel_row[2]) ** power[2]
                )
                for vel_row in velocity
            ]
            for power in exponents
        ]
    )
    inverse = invert_table(moments)
    opposite = [0, 2, 1, 4, 3, 6, 5, 8, 7, 10, 9, 12, 11, 14, 13, 16, 15, 18, 17]
    return (velocity, weights, moments, inverse, opposite)


def collide(populations, rates):
    velocity, weights, moments, inverse, opposite = tables()
    grid_shape = populations.shape
    columns = populations.reshape(19, -1)
    highest = lax.Precision.HIGHEST
    density = jnp.sum(columns, axis=0)
    momentum = jnp.dot(jnp.asarray(velocity.T, jnp.float32), columns, precision=highest)
    projected = jnp.dot(jnp.asarray(velocity, jnp.float32), momentum, precision=highest)
    momentum_sq = jnp.sum(momentum * momentum, axis=0)
    equilibrium = jnp.asarray(weights, jnp.float32)[:, None] * (
        density + 3.0 * projected + 4.5 * projected * projected - 1.5 * momentum_sq
    )
    kernel = jnp.dot(
        jnp.asarray(inverse, jnp.float32),
        rates[:, None] * jnp.asarray(moments, jnp.float32),
        precision=highest,
    )
    relaxed = columns - jnp.dot(kernel, columns - equilibrium, precision=highest)
    return relaxed.reshape(grid_shape)


def face_layer(extended, axis_dim, position):
    return lax.slice_in_dim(extended, position, position + 1, axis=axis_dim)


def section_x(extended):
    top_layer = face_layer(extended, 1, extended.shape[1] - 1)
    bottom_layer = face_layer(extended, 1, 0)
    from_below = from_behind(top_layer, "gx", 1)
    from_above = from_behind(bottom_layer, "gx", -1)
    return jnp.concatenate([from_below, extended, from_above], axis=1)


def section_y(extended):
    top_layer = face_layer(extended, 2, extended.shape[2] - 1)
    bottom_layer = face_layer(extended, 2, 0)
    from_below = from_behind(top_layer, "gy", 1)
    from_above = from_behind(bottom_layer, "gy", -1)
    return jnp.concatenate([from_below, extended, from_above], axis=2)


def section_z(extended):
    top_layer = face_layer(extended, 3, extended.shape[3] - 1)
    bottom_layer = face_layer(extended, 3, 0)
    from_below = from_behind(top_layer, "gz", 1)
    from_above = from_behind(bottom_layer, "gz", -1)
    return jnp.concatenate([from_below, extended, from_above], axis=3)


def stream(extended, flag_extended, relaxed, solid):
    velocity, weights, moments, inverse, opposite = tables()
    size_x, size_y, size_z = (relaxed.shape[1], relaxed.shape[2], relaxed.shape[3])
    outputs = []
    for index in range(19):
        start_x = 1 - int(velocity[index][0])
        start_y = 1 - int(velocity[index][1])
        start_z = 1 - int(velocity[index][2])
        source = extended[
            index,
            start_x : start_x + size_x,
            start_y : start_y + size_y,
            start_z : start_z + size_z,
        ]
        blocked = flag_extended[
            start_x : start_x + size_x, start_y : start_y + size_y, start_z : start_z + size_z
        ]
        value = jnp.where(blocked > 0.5, relaxed[opposite[index]], source)
        outputs.append(jnp.where(solid == 1, 0.0, value))
    return jnp.stack(outputs)


def shards(populations, solid, rates):
    solid_flag = solid.astype(jnp.float32)
    for time_step in range(STEPS):
        relaxed = collide(populations, rates)
        extended = jnp.concatenate([relaxed, solid_flag[None]], axis=0)
        extended = section_z(section_y(section_x(extended)))
        flag_extended = extended[19]
        populations = stream(extended, flag_extended, relaxed, solid)
    return populations


def solution(mesh):
    in_specs = (P(None, "gx", "gy", "gz"), P("gx", "gy", "gz"), P())
    out_specs = P(None, "gx", "gy", "gz")
    return jax.shard_map(shards, mesh=mesh, in_specs=in_specs, out_specs=out_specs, check_vma=False)
```

profile of v0, /device:TPU:0, one launch (start us, length us, event | category | flops | bytes accessed | tf_op | source)
XLA Modules:
  0.0 131.1 jit_solution(8012881412794263588)
XLA Ops:
  6.5 3.1 %collective-permute-start = (f32[20,1,16,128]{3,2,1,0:T(8,128)S(1)}, f32[20,1,16,128]{3,2,1,0:T(8,128)S(1)}, u32[]{:S(2)}, u32[]{:S(2)}) collective-permute-start(f32[20,1,16,128]{3,2,1,0:T(8,128)S(1)} %get-tuple-element.135), channel_id=1, source_target_pairs={{0,8},{8,16},{16,24},{24,0},{1,9},{9,17},{17,25},{25,1},{2,10},{10... | collective-permute-start | bytes 491528 | tf_op jit(solution)/shard_map/ppermute | solution.py:13
  9.6 2.1 %collective-permute-start.1 = (f32[20,1,16,128]{3,2,1,0:T(8,128)S(1)}, f32[20,1,16,128]{3,2,1,0:T(8,128)S(1)}, u32[]{:S(2)}, u32[]{:S(2)}) collective-permute-start(f32[20,1,16,128]{3,2,1,0:T(8,128)S(1)} %get-tuple-element.136), channel_id=1, source_target_pairs={{0,24},{8,0},{16,8},{24,16},{1,25},{9,1},{17,9},{25,17},{2,26},{10... | collective-permute-start | bytes 491528 | tf_op jit(solution)/shard_map/ppermute | solution.py:13
  11.7 5.0 %collective-permute-done = f32[20,1,16,128]{3,2,1,0:T(8,128)S(1)} collective-permute-done((f32[20,1,16,128]{3,2,1,0:T(8,128)S(1)}, f32[20,1,16,128]{3,2,1,0:T(8,128)S(1)}, u32[]{:S(2)}, u32[]{:S(2)}) %collective-permute-start) | collective-permute-done | bytes 163872 | tf_op jit(solution)/shard_map/ppermute | solution.py:13
  16.7 2.1 %collective-permute-done.1 = f32[20,1,16,128]{3,2,1,0:T(8,128)S(1)} collective-permute-done((f32[20,1,16,128]{3,2,1,0:T(8,128)S(1)}, f32[20,1,16,128]{3,2,1,0:T(8,128)S(1)}, u32[]{:S(2)}, u32[]{:S(2)}) %collective-permute-start.1) | collective-permute-done | bytes 163872 | tf_op jit(solution)/shard_map/ppermute | solution.py:13
  22.5 2.0 %collective-permute-done.2 = f32[20,6,1,128]{3,2,1,0:T(1,128)S(1)} collective-permute-done((f32[20,6,1,128]{3,2,1,0:T(1,128)S(1)}, f32[20,6,1,128]{3,2,1,0:T(1,128)S(1)}, u32[]{:S(2)}, u32[]{:S(2)}) %collective-permute-start.2) | collective-permute-done | bytes 61472 | tf_op jit(solution)/shard_map/ppermute | solution.py:13
  26.7 2.1 %copy.61 = f32[20,6,18,1]{0,3,2,1:T(1,128)S(1)} copy(f32[20,6,18,1]{3,2,1,0:T(8,128)} %get-tuple-element.54) | data formatting | bytes 17280 | tf_op jit(solution)/shard_map/slice | solution.py:118
  30.1 1.9 %fusion.41 = (f32[20,6,17,128]{3,2,1,0:T(8,128)}, f32[20,6,17,128]{3,2,1,0:T(8,128)}) fusion(f32[1,4,16,128]{3,2,1,0:T(8,128)S(1)} %convert_bitcast_fusion, f32[20,1,16,128]{3,2,1,0:T(8,128)S(1)} %collective-permute-done.1, f32[19,4,16,128]{3,2,1,0:T(8,128)S(1)} %bitcast.661, f32[20,1,16,128]{3,2,1,0:T(8,128)S(1)} %collective-permute-done, ...), kind=kLoop, calls=%fused_computation.66 | loop fusion | flops 2088960 | bytes 3194880 | tf_op jit(solution)/shard_map/concatenate | solution.py:134
  33.1 2.2 %copy.64 = f32[20,6,18,1]{3,2,1,0:T(8,128)} copy(f32[20,6,18,1]{0,3,2,1:T(1,128)S(1)} %collective-permute-done.5) | data formatting | bytes 17280 | tf_op jit(solution)/shard_map/ppermute | solution.py:13
  38.3 2.8 %fusion.4 = (f32[20,6,18,129]{3,2,1,0:T(8,128)S(1)}, f32[20,6,18,129]{3,2,1,0:T(8,128)S(1)}) fusion(f32[1,4,16,128]{3,2,1,0:T(8,128)S(1)} %convert_bitcast_fusion, f32[20,6,18,1]{3,2,1,0:T(8,128)S(1)} %copy-done, f32[20,6,1,128]{3,2,1,0:T(1,128)S(1)} %collective-permute-done.3, f32[20,1,16,128]{3,2,1,0:T(8,128)S(1)} %collective-permute-done.1, ...), kind=kLoop, calls=%fused_computation.13 | loop fusion | flops 3343680 | bytes 3352320 | tf_op jit(solution)/shard_map/concatenate | solution.py:142
  47.1 2.3 %collective-permute-start.7 = (f32[20,1,16,128]{3,2,1,0:T(8,128)S(1)}, f32[20,1,16,128]{3,2,1,0:T(8,128)S(1)}, u32[]{:S(2)}, u32[]{:S(2)}) collective-permute-start(f32[20,1,16,128]{3,2,1,0:T(8,128)S(1)} %get-tuple-element.134), channel_id=1, source_target_pairs={{0,24},{8,0},{16,8},{24,16},{1,25},{9,1},{17,9},{25,17},{2,26},{10... | collective-permute-start | bytes 491528 | tf_op jit(solution)/shard_map/ppermute | solution.py:13
  49.4 5.1 %collective-permute-done.6 = f32[20,1,16,128]{3,2,1,0:T(8,128)S(1)} collective-permute-done((f32[20,1,16,128]{3,2,1,0:T(8,128)S(1)}, f32[20,1,16,128]{3,2,1,0:T(8,128)S(1)}, u32[]{:S(2)}, u32[]{:S(2)}) %collective-permute-start.6) | collective-permute-done | bytes 163872 | tf_op jit(solution)/shard_map/ppermute | solution.py:13
  54.5 2.0 %collective-permute-done.7 = f32[20,1,16,128]{3,2,1,0:T(8,128)S(1)} collective-permute-done((f32[20,1,16,128]{3,2,1,0:T(8,128)S(1)}, f32[20,1,16,128]{3,2,1,0:T(8,128)S(1)}, u32[]{:S(2)}, u32[]{:S(2)}) %collective-permute-start.7) | collective-permute-done | bytes 163872 | tf_op jit(solution)/shard_map/ppermute | solution.py:13
  56.6 2.0 %collective-permute-start.8 = (f32[20,6,1,128]{3,2,1,0:T(1,128)S(1)}, f32[20,6,1,128]{3,2,1,0:T(1,128)S(1)}, u32[]{:S(2)}, u32[]{:S(2)}) collective-permute-start(f32[20,6,1,128]{3,2,1,0:T(1,128)S(1)} %get-tuple-element.68), channel_id=1, source_target_pairs={{0,2},{2,4},{4,6},{6,0},{1,3},{3,5},{5,7},{7,1},{8,10},{10,12},{12... | collective-permute-start | bytes 184328 | tf_op jit(solution)/shard_map/ppermute | solution.py:13
  64.7 2.1 %copy.67 = f32[20,6,18,1]{0,3,2,1:T(1,128)S(1)} copy(f32[20,6,18,1]{3,2,1,0:T(8,128)} %get-tuple-element.52) | data formatting | bytes 17280 | tf_op jit(solution)/shard_map/slice | solution.py:118
  68.1 1.9 %fusion.44 = (f32[20,6,17,128]{3,2,1,0:T(8,128)}, f32[20,6,17,128]{3,2,1,0:T(8,128)}) fusion(f32[1,4,16,128]{3,2,1,0:T(8,128)S(1)} %convert_bitcast_fusion, f32[20,1,16,128]{3,2,1,0:T(8,128)S(1)} %collective-permute-done.7, f32[19,4,16,128]{3,2,1,0:T(8,128)S(1)} %bitcast.668, f32[20,1,16,128]{3,2,1,0:T(8,128)S(1)} %collective-permute-done.6, ...), kind=kLoop, calls=%fused_computation.69 | loop fusion | flops 2088960 | bytes 3194880 | tf_op jit(solution)/shard_map/concatenate | solution.py:134
  71.1 2.2 %copy.70 = f32[20,6,18,1]{3,2,1,0:T(8,128)} copy(f32[20,6,18,1]{0,3,2,1:T(1,128)S(1)} %collective-permute-done.11) | data formatting | bytes 17280 | tf_op jit(solution)/shard_map/ppermute | solution.py:13
  76.3 2.8 %fusion.9 = (f32[20,6,18,129]{3,2,1,0:T(8,128)S(1)}, f32[20,6,18,129]{3,2,1,0:T(8,128)S(1)}) fusion(f32[1,4,16,128]{3,2,1,0:T(8,128)S(1)} %convert_bitcast_fusion, f32[20,6,18,1]{3,2,1,0:T(8,128)S(1)} %copy-done.1, f32[20,6,1,128]{3,2,1,0:T(1,128)S(1)} %collective-permute-done.9, f32[20,1,16,128]{3,2,1,0:T(8,128)S(1)} %collective-permute-done.7, ...), kind=kLoop, calls=%fused_computation.18 | loop fusion | flops 3343680 | bytes 3352320 | tf_op jit(solution)/shard_map/concatenate | solution.py:142
  83.4 2.1 %collective-permute-start.13 = (f32[20,1,16,128]{3,2,1,0:T(8,128)S(1)}, f32[20,1,16,128]{3,2,1,0:T(8,128)S(1)}, u32[]{:S(2)}, u32[]{:S(2)}) collective-permute-start(f32[20,1,16,128]{3,2,1,0:T(8,128)S(1)} %get-tuple-element.131), channel_id=1, source_target_pairs={{0,24},{8,0},{16,8},{24,16},{1,25},{9,1},{17,9},{25,17},{2,26},{10... | collective-permute-start | bytes 491528 | tf_op jit(solution)/shard_map/ppermute | solution.py:13
  86.1 4.0 %collective-permute-done.13 = f32[20,1,16,128]{3,2,1,0:T(8,128)S(1)} collective-permute-done((f32[20,1,16,128]{3,2,1,0:T(8,128)S(1)}, f32[20,1,16,128]{3,2,1,0:T(8,128)S(1)}, u32[]{:S(2)}, u32[]{:S(2)}) %collective-permute-start.13) | collective-permute-done | bytes 163872 | tf_op jit(solution)/shard_map/ppermute | solution.py:13
  90.1 4.0 %collective-permute-done.12 = f32[20,1,16,128]{3,2,1,0:T(8,128)S(1)} collective-permute-done((f32[20,1,16,128]{3,2,1,0:T(8,128)S(1)}, f32[20,1,16,128]{3,2,1,0:T(8,128)S(1)}, u32[]{:S(2)}, u32[]{:S(2)}) %collective-permute-start.12) | collective-permute-done | bytes 163872 | tf_op jit(solution)/shard_map/ppermute | solution.py:13
  101.9 2.1 %copy.73 = f32[20,6,18,1]{0,3,2,1:T(1,128)S(1)} copy(f32[20,6,18,1]{3,2,1,0:T(8,128)} %get-tuple-element.50) | data formatting | bytes 17280 | tf_op jit(solution)/shard_map/slice | solution.py:118
  105.3 1.8 %fusion.38 = (f32[20,6,17,128]{3,2,1,0:T(8,128)}, f32[20,6,17,128]{3,2,1,0:T(8,128)}) fusion(f32[1,4,16,128]{3,2,1,0:T(8,128)S(1)} %convert_bitcast_fusion, f32[20,6,1,128]{3,2,1,0:T(1,128)S(1)} %collective-permute-done.15, f32[20,1,16,128]{3,2,1,0:T(8,128)S(1)} %collective-permute-done.13, f32[19,4,16,128]{3,2,1,0:T(8,128)S(1)} %bitcast.653, ...), kind=kLoop, calls=%fused_computation.63 | loop fusion | flops 2088960 | bytes 3194880 | tf_op jit(solution)/shard_map/concatenate | solution.py:134
  108.2 2.2 %copy.76 = f32[20,6,18,1]{3,2,1,0:T(8,128)} copy(f32[20,6,18,1]{0,3,2,1:T(1,128)S(1)} %collective-permute-done.17) | data formatting | bytes 17280 | tf_op jit(solution)/shard_map/ppermute | solution.py:13
  115.8 2.8 %fusion.14 = (f32[20,6,18,129]{3,2,1,0:T(8,128)S(1)}, f32[20,6,18,129]{3,2,1,0:T(8,128)S(1)}) fusion(f32[1,4,16,128]{3,2,1,0:T(8,128)S(1)} %convert_bitcast_fusion, f32[20,6,18,1]{3,2,1,0:T(8,128)S(1)} %copy-done.2, f32[20,6,1,128]{3,2,1,0:T(1,128)S(1)} %collective-permute-done.15, f32[20,1,16,128]{3,2,1,0:T(8,128)S(1)} %collective-permute-done.13, ...), kind=kLoop, calls=%fused_computation.23 | loop fusion | flops 3343680 | bytes 3352320 | tf_op jit(solution)/shard_map/concatenate | solution.py:142
  (180 shorter events, 67.7 us)
Async XLA Ops:
  3.1 1.9 %copy-start.34 = (f32[19]{0:T(128)S(1)}, f32[19]{0:T(128)}, u32[]{:S(2)}) copy-start(f32[19]{0:T(128)} %param.20) | copy-start | bytes 232
  3.1 1.9 %copy-start.35 = (f32[19,19]{1,0:T(8,128)S(1)}, f32[19,19]{1,0:T(8,128)}, u32[]{:S(2)}) copy-start(f32[19,19]{1,0:T(8,128)} %constant.26.clone) | copy-start | bytes 4336
  3.1 2.2 %copy-start.5 = (f32[19]{0:T(128)S(1)}, f32[19]{0:T(128)}, u32[]{:S(2)}) copy-start(f32[19]{0:T(128)} %constant.24.clone) | copy-start | bytes 232
  6.5 10.2 %collective-permute-start = (f32[20,1,16,128]{3,2,1,0:T(8,128)S(1)}, f32[20,1,16,128]{3,2,1,0:T(8,128)S(1)}, u32[]{:S(2)}, u32[]{:S(2)}) collective-permute-start(f32[20,1,16,128]{3,2,1,0:T(8,128)S(1)} %get-tuple-element.135), channel_id=1, source_target_pairs={{0,8},{8,16},{16,24},{24,0},{1,9},{9,17},{17,25},{25,1},{2,10},{10... | collective-permute-start | bytes 491528 | tf_op jit(solution)/shard_map/ppermute | solution.py:13
  9.6 9.2 %collective-permute-start.1 = (f32[20,1,16,128]{3,2,1,0:T(8,128)S(1)}, f32[20,1,16,128]{3,2,1,0:T(8,128)S(1)}, u32[]{:S(2)}, u32[]{:S(2)}) collective-permute-start(f32[20,1,16,128]{3,2,1,0:T(8,128)S(1)} %get-tuple-element.136), channel_id=1, source_target_pairs={{0,24},{8,0},{16,8},{24,16},{1,25},{9,1},{17,9},{25,17},{2,26},{10... | collective-permute-start | bytes 491528 | tf_op jit(solution)/shard_map/ppermute | solution.py:13
  18.9 5.5 %collective-permute-start.2 = (f32[20,6,1,128]{3,2,1,0:T(1,128)S(1)}, f32[20,6,1,128]{3,2,1,0:T(1,128)S(1)}, u32[]{:S(2)}, u32[]{:S(2)}) collective-permute-start(f32[20,6,1,128]{3,2,1,0:T(1,128)S(1)} %get-tuple-element.72), channel_id=1, source_target_pairs={{0,2},{2,4},{4,6},{6,0},{1,3},{3,5},{5,7},{7,1},{8,10},{10,12},{12... | collective-permute-start | bytes 184328 | tf_op jit(solution)/shard_map/ppermute | solution.py:13
  20.5 4.3 %collective-permute-start.3 = (f32[20,6,1,128]{3,2,1,0:T(1,128)S(1)}, f32[20,6,1,128]{3,2,1,0:T(1,128)S(1)}, u32[]{:S(2)}, u32[]{:S(2)}) collective-permute-start(f32[20,6,1,128]{3,2,1,0:T(1,128)S(1)} %get-tuple-element.73), channel_id=1, source_target_pairs={{0,6},{2,0},{4,2},{6,4},{1,7},{3,1},{5,3},{7,5},{8,14},{10,8},{12,... | collective-permute-start | bytes 184328 | tf_op jit(solution)/shard_map/ppermute | solution.py:13
  29.5 3.5 %collective-permute-start.5 = (f32[20,6,18,1]{0,3,2,1:T(1,128)S(1)}, f32[20,6,18,1]{0,3,2,1:T(1,128)S(1)}, u32[]{:S(2)}, u32[]{:S(2)}) collective-permute-start(f32[20,6,18,1]{0,3,2,1:T(1,128)S(1)} %copy.62), channel_id=1, source_target_pairs={{0,1},{1,0},{2,3},{3,2},{4,5},{5,4},{6,7},{7,6},{8,9},{9,8},{10,11... | collective-permute-start | bytes 25928 | tf_op jit(solution)/shard_map/ppermute | solution.py:13
  29.6 2.4 %collective-permute-start.4 = (f32[20,6,18,1]{0,3,2,1:T(1,128)S(1)}, f32[20,6,18,1]{0,3,2,1:T(1,128)S(1)}, u32[]{:S(2)}, u32[]{:S(2)}) collective-permute-start(f32[20,6,18,1]{0,3,2,1:T(1,128)S(1)} %copy.61), channel_id=1, source_target_pairs={{0,1},{1,0},{2,3},{3,2},{4,5},{5,4},{6,7},{7,6},{8,9},{9,8},{10,11... | collective-permute-start | bytes 25928 | tf_op jit(solution)/shard_map/ppermute | solution.py:13
  36.3 2.0 %copy-start = (f32[20,6,18,1]{3,2,1,0:T(8,128)S(1)}, f32[20,6,18,1]{3,2,1,0:T(8,128)}, u32[]{:S(2)}) copy-start(f32[20,6,18,1]{3,2,1,0:T(8,128)} %copy.64) | copy-start | bytes 25924
  45.5 9.0 %collective-permute-start.6 = (f32[20,1,16,128]{3,2,1,0:T(8,128)S(1)}, f32[20,1,16,128]{3,2,1,0:T(8,128)S(1)}, u32[]{:S(2)}, u32[]{:S(2)}) collective-permute-start(f32[20,1,16,128]{3,2,1,0:T(8,128)S(1)} %get-tuple-element.133), channel_id=1, source_target_pairs={{0,8},{8,16},{16,24},{24,0},{1,9},{9,17},{17,25},{25,1},{2,10},{10... | collective-permute-start | bytes 491528 | tf_op jit(solution)/shard_map/ppermute | solution.py:13
  47.1 9.4 %collective-permute-start.7 = (f32[20,1,16,128]{3,2,1,0:T(8,128)S(1)}, f32[20,1,16,128]{3,2,1,0:T(8,128)S(1)}, u32[]{:S(2)}, u32[]{:S(2)}) collective-permute-start(f32[20,1,16,128]{3,2,1,0:T(8,128)S(1)} %get-tuple-element.134), channel_id=1, source_target_pairs={{0,24},{8,0},{16,8},{24,16},{1,25},{9,1},{17,9},{25,17},{2,26},{10... | collective-permute-start | bytes 491528 | tf_op jit(solution)/shard_map/ppermute | solution.py:13
  56.6 5.2 %collective-permute-start.8 = (f32[20,6,1,128]{3,2,1,0:T(1,128)S(1)}, f32[20,6,1,128]{3,2,1,0:T(1,128)S(1)}, u32[]{:S(2)}, u32[]{:S(2)}) collective-permute-start(f32[20,6,1,128]{3,2,1,0:T(1,128)S(1)} %get-tuple-element.68), channel_id=1, source_target_pairs={{0,2},{2,4},{4,6},{6,0},{1,3},{3,5},{5,7},{7,1},{8,10},{10,12},{12... | collective-permute-start | bytes 184328 | tf_op jit(solution)/shard_map/ppermute | solution.py:13
  58.6 4.2 %collective-permute-start.9 = (f32[20,6,1,128]{3,2,1,0:T(1,128)S(1)}, f32[20,6,1,128]{3,2,1,0:T(1,128)S(1)}, u32[]{:S(2)}, u32[]{:S(2)}) collective-permute-start(f32[20,6,1,128]{3,2,1,0:T(1,128)S(1)} %get-tuple-element.69), channel_id=1, source_target_pairs={{0,6},{2,0},{4,2},{6,4},{1,7},{3,1},{5,3},{7,5},{8,14},{10,8},{12,... | collective-permute-start | bytes 184328 | tf_op jit(solution)/shard_map/ppermute | solution.py:13
  67.6 3.5 %collective-permute-start.11 = (f32[20,6,18,1]{0,3,2,1:T(1,128)S(1)}, f32[20,6,18,1]{0,3,2,1:T(1,128)S(1)}, u32[]{:S(2)}, u32[]{:S(2)}) collective-permute-start(f32[20,6,18,1]{0,3,2,1:T(1,128)S(1)} %copy.68), channel_id=1, source_target_pairs={{0,1},{1,0},{2,3},{3,2},{4,5},{5,4},{6,7},{7,6},{8,9},{9,8},{10,11... | collective-permute-start | bytes 25928 | tf_op jit(solution)/shard_map/ppermute | solution.py:13
  67.6 2.4 %collective-permute-start.10 = (f32[20,6,18,1]{0,3,2,1:T(1,128)S(1)}, f32[20,6,18,1]{0,3,2,1:T(1,128)S(1)}, u32[]{:S(2)}, u32[]{:S(2)}) collective-permute-start(f32[20,6,18,1]{0,3,2,1:T(1,128)S(1)} %copy.67), channel_id=1, source_target_pairs={{0,1},{1,0},{2,3},{3,2},{4,5},{5,4},{6,7},{7,6},{8,9},{9,8},{10,11... | collective-permute-start | bytes 25928 | tf_op jit(solution)/shard_map/ppermute | solution.py:13
  74.3 2.0 %copy-start.1 = (f32[20,6,18,1]{3,2,1,0:T(8,128)S(1)}, f32[20,6,18,1]{3,2,1,0:T(8,128)}, u32[]{:S(2)}) copy-start(f32[20,6,18,1]{3,2,1,0:T(8,128)} %copy.70) | copy-start | bytes 25924
  83.4 6.8 %collective-permute-start.13 = (f32[20,1,16,128]{3,2,1,0:T(8,128)S(1)}, f32[20,1,16,128]{3,2,1,0:T(8,128)S(1)}, u32[]{:S(2)}, u32[]{:S(2)}) collective-permute-start(f32[20,1,16,128]{3,2,1,0:T(8,128)S(1)} %get-tuple-element.131), channel_id=1, source_target_pairs={{0,24},{8,0},{16,8},{24,16},{1,25},{9,1},{17,9},{25,17},{2,26},{10... | collective-permute-start | bytes 491528 | tf_op jit(solution)/shard_map/ppermute | solution.py:13
  85.5 8.6 %collective-permute-start.12 = (f32[20,1,16,128]{3,2,1,0:T(8,128)S(1)}, f32[20,1,16,128]{3,2,1,0:T(8,128)S(1)}, u32[]{:S(2)}, u32[]{:S(2)}) collective-permute-start(f32[20,1,16,128]{3,2,1,0:T(8,128)S(1)} %get-tuple-element.132), channel_id=1, source_target_pairs={{0,8},{8,16},{16,24},{24,0},{1,9},{9,17},{17,25},{25,1},{2,10},{10... | collective-permute-start | bytes 491528 | tf_op jit(solution)/shard_map/ppermute | solution.py:13
  94.3 5.2 %collective-permute-start.14 = (f32[20,6,1,128]{3,2,1,0:T(1,128)S(1)}, f32[20,6,1,128]{3,2,1,0:T(1,128)S(1)}, u32[]{:S(2)}, u32[]{:S(2)}) collective-permute-start(f32[20,6,1,128]{3,2,1,0:T(1,128)S(1)} %get-tuple-element.64), channel_id=1, source_target_pairs={{0,2},{2,4},{4,6},{6,0},{1,3},{3,5},{5,7},{7,1},{8,10},{10,12},{12... | collective-permute-start | bytes 184328 | tf_op jit(solution)/shard_map/ppermute | solution.py:13
  95.8 4.2 %collective-permute-start.15 = (f32[20,6,1,128]{3,2,1,0:T(1,128)S(1)}, f32[20,6,1,128]{3,2,1,0:T(1,128)S(1)}, u32[]{:S(2)}, u32[]{:S(2)}) collective-permute-start(f32[20,6,1,128]{3,2,1,0:T(1,128)S(1)} %get-tuple-element.65), channel_id=1, source_target_pairs={{0,6},{2,0},{4,2},{6,4},{1,7},{3,1},{5,3},{7,5},{8,14},{10,8},{12,... | collective-permute-start | bytes 184328 | tf_op jit(solution)/shard_map/ppermute | solution.py:13
  104.8 3.5 %collective-permute-start.17 = (f32[20,6,18,1]{0,3,2,1:T(1,128)S(1)}, f32[20,6,18,1]{0,3,2,1:T(1,128)S(1)}, u32[]{:S(2)}, u32[]{:S(2)}) collective-permute-start(f32[20,6,18,1]{0,3,2,1:T(1,128)S(1)} %copy.74), channel_id=1, source_target_pairs={{0,1},{1,0},{2,3},{3,2},{4,5},{5,4},{6,7},{7,6},{8,9},{9,8},{10,11... | collective-permute-start | bytes 25928 | tf_op jit(solution)/shard_map/ppermute | solution.py:13
  104.8 2.3 %collective-permute-start.16 = (f32[20,6,18,1]{0,3,2,1:T(1,128)S(1)}, f32[20,6,18,1]{0,3,2,1:T(1,128)S(1)}, u32[]{:S(2)}, u32[]{:S(2)}) collective-permute-start(f32[20,6,18,1]{0,3,2,1:T(1,128)S(1)} %copy.73), channel_id=1, source_target_pairs={{0,1},{1,0},{2,3},{3,2},{4,5},{5,4},{6,7},{7,6},{8,9},{9,8},{10,11... | collective-permute-start | bytes 25928 | tf_op jit(solution)/shard_map/ppermute | solution.py:13
  111.4 4.4 %copy-start.2 = (f32[20,6,18,1]{3,2,1,0:T(8,128)S(1)}, f32[20,6,18,1]{3,2,1,0:T(8,128)}, u32[]{:S(2)}) copy-start(f32[20,6,18,1]{3,2,1,0:T(8,128)} %copy.76) | copy-start | bytes 25924
  (31 other events, 24.1 us)
where the time goes:
time: 132 us; the launch traced here: 131 us
  other arithmetic  43 us (33%)
  local copies, waits for them, and re-layouts  30.1 us (23%)
  waiting for transfers between devices  29.4 us (22%)
  starting transfers between devices  21.8 us (17%)
  matrix products  6.09 us (5%)
    ppermute x18, waiting for transfers between devices, from_behind(): return lax.ppermute(value, axis, pairs)  29.4 us
    ppermute x18, starting transfers between devices, from_behind(): return lax.ppermute(value, axis, pairs)  21.8 us
    unnamed x18, other arithmetic  16.9 us
    slice x12, local copies, waits for them, and re-layouts, face_layer(): return lax.slice_in_dim(extended, position, position + 1, axis=axis_dim)  13.7 us
    ppermute x6, local copies, waits for them, and re-layouts, from_behind(): return lax.ppermute(value, axis, pairs)  9.73 us
    concatenate x3, other arithmetic, section_z(): return jnp.concatenate([from_below, extended, from_above], axis=3)  8.42 us
    concatenate x6, other arithmetic, section_y(): return jnp.concatenate([from_below, extended, from_above], axis=2)  6.28 us
    reduce_sum x5, other arithmetic, collide(): density = jnp.sum(columns, axis=0)  3.25 us
  transfers between devices with their start and end apart: 18, of which 12 were waited for; matrix products, arithmetic and copies ran while one was open for 8% of the time, Pallas kernels for 0%

commit v1 on v0

v1 whole, which is shorter than its diff:
```python
import functools

import jax
import jax.numpy as jnp
from jax import lax
from jax.experimental import pallas as pl
from jax.experimental.pallas import tpu as pltpu
from jax.sharding import PartitionSpec as P

STEPS = 3
VELOCITY = [
    (0, 0, 0), (1, 0, 0), (-1, 0, 0), (0, 1, 0), (0, -1, 0), (0, 0, 1), (0, 0, -1),
    (1, 1, 0), (-1, -1, 0), (1, -1, 0), (-1, 1, 0),
    (1, 0, 1), (-1, 0, -1), (1, 0, -1), (-1, 0, 1),
    (0, 1, 1), (0, -1, -1), (0, 1, -1), (0, -1, 1),
]
OPPOSITE = [0, 2, 1, 4, 3, 6, 5, 8, 7, 10, 9, 12, 11, 14, 13, 16, 15, 18, 17]
X_OUT = ([1, 7, 9, 11, 13], [2, 8, 10, 12, 14])
Y_OUT = ([3, 7, 10, 15, 17], [4, 8, 9, 16, 18])
EDGE = [7, 8, 9, 10]
MESH = pl.DeviceIdType.MESH


def collide(f, rate):
    pairs = [(index, index + 1) for index in range(1, 19, 2)]
    total = [f[a] + f[b] for a, b in pairs]
    diff = [f[a] - f[b] for a, b in pairs]
    density = f[0] + ((total[0] + total[1] + total[2]) + (total[3] + total[4])
                      + (total[5] + total[6]) + (total[7] + total[8]))
    jx = diff[0] + (diff[3] + diff[4]) + (diff[5] + diff[6])
    jy = diff[1] + (diff[3] - diff[4]) + (diff[7] + diff[8])
    jz = diff[2] + (diff[5] - diff[6]) + (diff[7] - diff[8])
    base = density - 1.5 * (jx * jx + jy * jy + jz * jz)
    projected = [jx, jy, jz, jx + jy, jx - jy, jx + jz, jx - jz, jy + jz, jy - jz]
    rest = f[0] - (1.0 / 3.0) * base
    even, odd = [], []
    for k in range(9):
        weight = 1.0 / 18.0 if k < 3 else 1.0 / 36.0
        p = projected[k]
        even.append(total[k] - (2.0 * weight) * (base + 4.5 * (p * p)))
        odd.append(diff[k] - (6.0 * weight) * p)
    xxyy, xxzz, yyzz = even[3] + even[4], even[5] + even[6], even[7] + even[8]
    xyy, xzz, yzz = odd[3] + odd[4], odd[5] + odd[6], odd[7] + odd[8]
    xxy, xxz, yyz = odd[3] - odd[4], odd[5] - odd[6], odd[7] - odd[8]
    one = rate[0] * (rest + ((even[0] + even[1] + even[2]) + (xxyy + xxzz + yyzz)))
    mx = rate[1] * (odd[0] + xyy + xzz)
    my = rate[2] * (odd[1] + xxy + yzz)
    mz = rate[3] * (odd[2] + xxz + yyz)
    xx = rate[4] * (even[0] + xxyy + xxzz)
    yy = rate[5] * (even[1] + xxyy + yyzz)
    zz = rate[6] * (even[2] + xxzz + yyzz)
    xy = rate[7] * (even[3] - even[4])
    xz = rate[8] * (even[5] - even[6])
    yz = rate[9] * (even[7] - even[8])
    xxy, xxz, xyy = rate[10] * xxy, rate[11] * xxz, rate[12] * xyy
    yyz, xzz, yzz = rate[13] * yyz, rate[14] * xzz, rate[15] * yzz
    xxyy, xxzz, yyzz = rate[16] * xxyy, rate[17] * xxzz, rate[18] * yyzz
    change = [None] * 19
    change[0] = one - (xx + yy + zz) + (xxyy + xxzz + yyzz)
    sums = [xx - xxyy - xxzz, yy - xxyy - yyzz, zz - xxzz - yyzz]
    diffs = [mx - xyy - xzz, my - xxy - yzz, mz - xxz - yyz]
    for k in range(3):
        change[1 + 2 * k] = 0.5 * (sums[k] + diffs[k])
        change[2 + 2 * k] = 0.5 * (sums[k] - diffs[k])
    for k, (s, d, a, b) in enumerate(
        [(xxyy, xy, xyy, xxy), (xxzz, xz, xzz, xxz), (yyzz, yz, yzz, yyz)]
    ):
        plus, minus = 0.25 * (s + d), 0.25 * (s - d)
        up, down = 0.25 * (a + b), 0.25 * (a - b)
        change[7 + 4 * k] = plus + up
        change[8 + 4 * k] = plus - up
        change[9 + 4 * k] = minus + down
        change[10 + 4 * k] = minus - down
    return [f[index] - change[index] for index in range(19)]


def kernel(sizes, pop, sol, rates, out, held, relaxed, flag, blocked, xs, xr, ys, yr, es, er,
           osend, iflag, own_sem, in_send, in_recv, x_send, x_recv, y_send, y_recv, e_send, e_recv,
           o_send, o_recv):
    gxn, gyn, gzn, nx, ny = sizes
    pair = gzn == 2
    gx, gy, gz = lax.axis_index("gx"), lax.axis_index("gy"), lax.axis_index("gz")
    row_block = gy * gzn + gz

    def device(dx, dy):
        block = lax.rem(row_block + dy + gyn * gzn, gyn * gzn)
        return (lax.rem(gx + dx + gxn, gxn), block // gzn, lax.rem(block, gzn))

    order = [0, nx - 1] + list(range(1, nx - 1))
    local = []
    if pair:
        other = (gx, gy, 1 - gz)
        mine = pl.ds(pl.multiple_of(gz * ny, ny), ny)
        others = pl.ds(pl.multiple_of((1 - gz) * ny, ny), ny)
        for x in order:
            local.append(pltpu.make_async_copy(
                pop.at[:, x, mine, :], held.at[:, x, gz], own_sem.at[x]))
        local.append(pltpu.make_async_copy(sol.at[:, mine, :], iflag.at[:, gz], own_sem.at[nx]))
    else:
        for x in order:
            local.append(pltpu.make_async_copy(pop.at[:, x], held.at[:, x], own_sem.at[x]))
        local.append(pltpu.make_async_copy(sol, iflag, own_sem.at[nx]))
    for copy in local:
        copy.start()

    barrier = pltpu.get_barrier_semaphore()
    around = [(dx, dy) for dx in (-1, 0, 1) for dy in (-1, 0, 1) if (dx, dy) != (0, 0)]
    for dx, dy in around:
        pl.semaphore_signal(barrier, inc=1, device_id=device(dx, dy), device_id_type=MESH)
    pl.semaphore_wait(barrier, len(around))

    def remote(src, dst, send, recv, to):
        copy = pltpu.make_async_remote_copy(
            src_ref=src, dst_ref=dst, send_sem=send, recv_sem=recv,
            device_id=to, device_id_type=MESH)
        copy.start()
        return copy

    moved = []
    if pair:
        for x in order:
            moved.append(remote(pop.at[:, x, others, :], held.at[:, x, gz],
                                in_send.at[x], in_recv.at[x], other))
        moved.append(remote(sol.at[:, others, :], iflag.at[:, gz],
                            in_send.at[nx], in_recv.at[nx], other))

    shape = (gzn, ny, 128)
    row = lax.broadcasted_iota(jnp.int32, shape, 1)
    lane = lax.broadcasted_iota(jnp.int32, shape, 2)
    rate = [rates[index] for index in range(19)]
    sent = list(moved)

    def arrived(index):
        local[index].wait()
        if pair:
            moved[index].wait_recv()

    def shifted(plane, halo, velocity):
        cx, cy, cz = velocity
        value = plane()
        if cy:
            value = jnp.where(row == (0 if cy > 0 else ny - 1),
                              jnp.broadcast_to(halo(), shape), pltpu.roll(value, cy % ny, 1))
        if cz:
            turned = pltpu.roll(value, cz % 128, 2)
            if cz > 0:
                swapped = jnp.concatenate([turned[-1:], turned[:-1]], axis=0)
            else:
                swapped = jnp.concatenate([turned[1:], turned[:1]], axis=0)
            value = jnp.where(lane == (0 if cz > 0 else 127), swapped, turned)
        return value

    def source(t, p, x, is_flag):
        cx, cy, cz = VELOCITY[p]
        sx = x - cx
        outside = sx < 0 or sx >= nx
        xd, yd = (0 if cx > 0 else 1), (0 if cy > 0 else 1)

        def plane():
            if outside:
                return xr[t, xd, 5 if is_flag else X_OUT[xd].index(p)]
            return flag[sx] if is_flag else relaxed[p, sx]

        def halo():
            if outside:
                return er[t, EDGE.index(p), 1 if is_flag else 0]
            return yr[t, yd, 5 if is_flag else Y_OUT[yd].index(p), sx]

        return shifted(plane, halo, (cx, cy, cz))

    for t in range(STEPS):
        last = t == STEPS - 1
        if t == 0:
            arrived(nx)
            for x in range(nx):
                flag[x] = iflag[x].astype(jnp.float32)
                for d, at in ((0, ny - 1), (1, 0)):
                    ys[0, d, 5, x] = flag[x, :, at : at + 1, :]
            xs[0, 0, 5] = flag[nx - 1]
            xs[0, 1, 5] = flag[0]
            for e, p in enumerate(EDGE):
                cx, cy, _ = VELOCITY[p]
                at = ny - 1 if cy > 0 else 0
                es[0, e, 1] = flag[nx - 1 if cx > 0 else 0, :, at : at + 1, :]
        count = 6 if t == 0 else 5
        ecount = 2 if t == 0 else 1
        x_copies, e_copies, y_copies = [], [], []
        for place, x in enumerate(order):
            if t == 0:
                arrived(place)
            values = collide([held[index, x] for index in range(19)], rate)
            for index in range(19):
                relaxed[index, x] = values[index]
            for d, at in ((0, ny - 1), (1, 0)):
                for k, p in enumerate(Y_OUT[d]):
                    ys[t, d, k, x] = values[p][:, at : at + 1, :]
            d = {nx - 1: 0, 0: 1}.get(x)
            if d is not None:
                for k, p in enumerate(X_OUT[d]):
                    xs[t, d, k] = values[p]
                x_copies.append(remote(
                    xs.at[t, d, pl.ds(0, count)], xr.at[t, d, pl.ds(0, count)],
                    x_send.at[t, d], x_recv.at[t, d], device(1 if d == 0 else -1, 0)))
                for e, p in enumerate(EDGE):
                    cx, cy, _ = VELOCITY[p]
                    if (cx > 0) == (d == 0):
                        at = ny - 1 if cy > 0 else 0
                        es[t, e, 0] = values[p][:, at : at + 1, :]
                        e_copies.append(remote(
                            es.at[t, e, pl.ds(0, ecount)], er.at[t, e, pl.ds(0, ecount)],
                            e_send.at[t, e], e_recv.at[t, e], device(cx, cy)))
        for d in (0, 1):
            y_copies.append(remote(
                ys.at[t, d, pl.ds(0, count)], yr.at[t, d, pl.ds(0, count)],
                y_send.at[t, d], y_recv.at[t, d], device(0, 1 if d == 0 else -1)))
        sent += x_copies + e_copies + y_copies
        for copy in y_copies:
            copy.wait_recv()
        for place, x in enumerate(order[2:] + order[:2]):
            if place == nx - 2:
                for copy in x_copies + e_copies:
                    copy.wait_recv()
            rock = flag[x] > 0.5
            for p in range(19):
                if p == 0:
                    value = relaxed[0, x]
                else:
                    if t == 0:
                        wall = source(0, p, x, True)
                        blocked[p, x] = wall
                    else:
                        wall = blocked[p, x]
                    value = jnp.where(wall > 0.5, relaxed[OPPOSITE[p], x], source(t, p, x, False))
                value = jnp.where(rock, 0.0, value)
                if not last:
                    held[p, x] = value
                elif pair:
                    first = gz == 0
                    out[p, x, mine, :] = jnp.where(first, value[0], value[1])
                    osend[p, x] = jnp.where(first, value[1], value[0])
                else:
                    out[p, x] = value
            if last and pair:
                copy = remote(osend.at[:, x], out.at[:, x, mine, :],
                              o_send.at[x], o_recv.at[x], other)
                sent.append(copy)
                moved.append(copy)
    if pair:
        for copy in moved[nx + 1:]:
            copy.wait_recv()
    for copy in sent:
        copy.wait_send()


def shards(sizes, populations, solid, rates):
    gxn, gyn, gzn, nx, ny = sizes
    pair = gzn == 2
    if not pair:
        populations = lax.all_to_all(
            populations.reshape(19, nx, gzn, ny, 128), "gz", 2, 2, tiled=True)
        solid = lax.all_to_all(solid.reshape(nx, gzn, ny, 128), "gz", 1, 1, tiled=True)
    f32, dma, vmem = jnp.float32, pltpu.SemaphoreType.DMA, pltpu.VMEM
    block = (gzn, ny, 128)
    line = (gzn, 1, 128)
    out = pl.pallas_call(
        functools.partial(kernel, sizes),
        out_shape=jax.ShapeDtypeStruct(populations.shape, f32),
        in_specs=[
            pl.BlockSpec(memory_space=pl.ANY),
            pl.BlockSpec(memory_space=pl.ANY),
            pl.BlockSpec(memory_space=pltpu.SMEM),
        ],
        out_specs=pl.BlockSpec(memory_space=pltpu.VMEM),
        scratch_shapes=[
            vmem((19, nx) + block, f32),
            vmem((19, nx) + block, f32),
            vmem((nx,) + block, f32),
            vmem((19, nx) + block, f32),
            vmem((STEPS, 2, 6) + block, f32),
            vmem((STEPS, 2, 6) + block, f32),
            vmem((STEPS, 2, 6, nx) + line, f32),
            vmem((STEPS, 2, 6, nx) + line, f32),
            vmem((STEPS, 4, 2) + line, f32),
            vmem((STEPS, 4, 2) + line, f32),
            vmem((19, nx, ny, 128), f32),
            vmem((nx,) + block, jnp.int32),
            dma((nx + 1,)),
            dma((nx + 1,)),
            dma((nx + 1,)),
            dma((STEPS, 2)),
            dma((STEPS, 2)),
            dma((STEPS, 2)),
            dma((STEPS, 2)),
            dma((STEPS, 4)),
            dma((STEPS, 4)),
            dma((nx,)),
            dma((nx,)),
        ],
        compiler_params=pltpu.CompilerParams(
            collective_id=0, has_side_effects=True, vmem_limit_bytes=32 * 1024 * 1024),
    )(populations, solid, rates)
    if not pair:
        out = lax.all_to_all(out, "gz", 2, 2, tiled=True).reshape(19, nx, gzn * ny, 128)
    return out


def solution(mesh):
    gxn, gyn, gzn = mesh.shape["gx"], mesh.shape["gy"], mesh.shape["gz"]

    def run(populations, solid, rates):
        sizes = (gxn, gyn, gzn, populations.shape[1] // gxn, populations.shape[2] // (gyn * gzn))
        in_specs = (P(None, "gx", "gy", "gz"), P("gx", "gy", "gz"), P())
        out_specs = P(None, "gx", "gy", "gz")
        return jax.shard_map(functools.partial(shards, sizes), mesh=mesh, in_specs=in_specs,
                             out_specs=out_specs, check_vma=False)(populations, solid, rates)

    return run
```

time: 132 us -> 28.5 us (0.22)
  other arithmetic: 43 us -> 0 us
  waiting for transfers between devices: 29.4 us -> 0 us
  local copies, waits for them, and re-layouts: 30.1 us -> 3.32 us
  Pallas kernels: 0 us -> 24.9 us
  starting transfers between devices: 21.8 us -> 0 us
  matrix products: 6.09 us -> 0 us
    ppermute x18 -> x0, waiting for transfers between devices: 29.4 us -> none  [from_behind(): return lax.ppermute(value, axis, pairs)]
    pallas_call x0 -> x1, Pallas kernels: none -> 24.9 us  [shards(): pl.pallas_call(functools.partial(kernel, sizes), out_shape=jax.ShapeDtype...]
    ppermute x18 -> x0, starting transfers between devices: 21.8 us -> none  [from_behind(): return lax.ppermute(value, axis, pairs)]
    unnamed x18 -> x0, other arithmetic: 16.9 us -> none
    slice x15 -> x0, local copies, waits for them, and re-layouts: 15.4 us -> none  [the longest x12 13.7 us: face_layer(): return lax.slice_in_dim(extended, position, position + 1, axis=axis_dim)]
    concatenate x15 -> x0, other arithmetic: 15 us -> none  [the longest x3 8.42 us: section_z(): return jnp.concatenate([from_below, extended, from_above], axis=3)]
    ppermute x6 -> x0, local copies, waits for them, and re-layouts: 9.73 us -> none  [from_behind(): return lax.ppermute(value, axis, pairs)]
    dot_general x8 -> x0, matrix products: 6.09 us -> none  [the longest x3 2.98 us: collide(): jnp.dot(kernel, columns - equilibrium, precision=highest)]
  transfers between devices with their start and end apart: 18 -> 0, of which waited for: 12 -> 0; matrix products, arithmetic and copies ran while one was open for 8% -> 0% of each run, Pallas kernels for 0% -> 0%
where the time goes in v1:
time: 28.5 us; the launch traced here: 28.2 us
  Pallas kernels  24.9 us (87%)
  local copies, waits for them, and re-layouts  3.32 us (12%)
    pallas_call x1, Pallas kernels, shards(): pl.pallas_call(functools.partial(kernel, sizes), out_shape=jax.ShapeDtype...  24.9 us
    unnamed x7, local copies, waits for them, and re-layouts  3.32 us

profile of v1, /device:TPU:0, one launch (start us, length us, event | category | flops | bytes accessed | tf_op | source)
XLA Modules:
  0.0 28.2 jit_solution(7776452482807014915)
XLA Ops:
  0.0 0.0 copy-start
  0.0 1.1 %copy-done = f32[19,4,16,128]{3,2,1,0:T(8,128)S(1)} copy-done((f32[19,4,16,128]{3,2,1,0:T(8,128)S(1)}, f32[19,4,16,128]{3,2,1,0:T(8,128)}, u32[]{:S(2)}) %copy-start) | copy-done | bytes 622616
  1.1 0.0 copy-start.1
  1.1 0.8 %copy-done.1 = s32[4,16,128]{2,1,0:T(8,128)S(1)} copy-done((s32[4,16,128]{2,1,0:T(8,128)S(1)}, s32[4,16,128]{2,1,0:T(8,128)}, u32[]{:S(2)}) %copy-start.1) | copy-done | bytes 32792
  1.8 0.0 copy-start.2
  1.8 0.7 %copy-done.2 = f32[19]{0:T(128)S(1)} copy-done((f32[19]{0:T(128)S(1)}, f32[19]{0:T(128)}, u32[]{:S(2)}) %copy-start.2) | copy-done | bytes 100
  2.5 24.9 %shard_map.37 = f32[19,4,16,128]{3,2,1,0:T(8,128)S(1)} custom-call(f32[19,4,16,128]{3,2,1,0:T(8,128)S(1)} %copy-done, s32[4,16,128]{2,1,0:T(8,128)S(1)} %copy-done.1, f32[19]{0:T(128)S(1)} %copy-done.2), custom_call_target="tpu_custom_call" | custom-call | tf_op jit(solution)/shard_map/pallas_call | solution.py:265
  27.4 0.8 %copy.5 = f32[19,4,16,128]{3,2,1,0:T(8,128)} copy(f32[19,4,16,128]{3,2,1,0:T(8,128)S(1)} %shard_map.37) | data formatting | bytes 1245184
Async XLA Ops:
  0.0 1.1 %copy-start = (f32[19,4,16,128]{3,2,1,0:T(8,128)S(1)}, f32[19,4,16,128]{3,2,1,0:T(8,128)}, u32[]{:S(2)}) copy-start(f32[19,4,16,128]{3,2,1,0:T(8,128)} %pop.1) | copy-start | bytes 1867780
  1.1 0.8 %copy-start.1 = (s32[4,16,128]{2,1,0:T(8,128)S(1)}, s32[4,16,128]{2,1,0:T(8,128)}, u32[]{:S(2)}) copy-start(s32[4,16,128]{2,1,0:T(8,128)} %sol.1) | copy-start | bytes 98308
  1.8 0.7 %copy-start.2 = (f32[19]{0:T(128)S(1)}, f32[19]{0:T(128)}, u32[]{:S(2)}) copy-start(f32[19]{0:T(128)} %rates.1) | copy-start | bytes 232

commit v2 on v1

--- a/solution.py
+++ b/solution.py
@@ -74,8 +74,8 @@
     return [f[index] - change[index] for index in range(19)]
 
 
-def kernel(sizes, pop, sol, rates, out, held, relaxed, flag, blocked, xs, xr, ys, yr, es, er,
-           osend, iflag, own_sem, in_send, in_recv, x_send, x_recv, y_send, y_recv, e_send, e_recv,
+def kernel(sizes, pop, sol, rates_in, out, held, relaxed, flag, blocked, xs, xr, ys, yr, es, er,
+           osend, iflag, rates, own_sem, in_send, in_recv, x_send, x_recv, y_send, y_recv, e_send, e_recv,
            o_send, o_recv):
     gxn, gyn, gzn, nx, ny = sizes
     pair = gzn == 2
@@ -88,6 +88,8 @@
 
     order = [0, nx - 1] + list(range(1, nx - 1))
     local = []
+    rates_copy = pltpu.make_async_copy(rates_in, rates, own_sem.at[nx + 1])
+    rates_copy.start()
     if pair:
         other = (gx, gy, 1 - gz)
         mine = pl.ds(pl.multiple_of(gz * ny, ny), ny)
@@ -127,6 +129,7 @@
     shape = (gzn, ny, 128)
     row = lax.broadcasted_iota(jnp.int32, shape, 1)
     lane = lax.broadcasted_iota(jnp.int32, shape, 2)
+    rates_copy.wait()
     rate = [rates[index] for index in range(19)]
     sent = list(moved)
 
@@ -196,11 +199,6 @@
                     ys[t, d, k, x] = values[p][:, at : at + 1, :]
             d = {nx - 1: 0, 0: 1}.get(x)
             if d is not None:
-                for k, p in enumerate(X_OUT[d]):
-                    xs[t, d, k] = values[p]
-                x_copies.append(remote(
-                    xs.at[t, d, pl.ds(0, count)], xr.at[t, d, pl.ds(0, count)],
-                    x_send.at[t, d], x_recv.at[t, d], device(1 if d == 0 else -1, 0)))
                 for e, p in enumerate(EDGE):
                     cx, cy, _ = VELOCITY[p]
                     if (cx > 0) == (d == 0):
@@ -209,6 +207,14 @@
                         e_copies.append(remote(
                             es.at[t, e, pl.ds(0, ecount)], er.at[t, e, pl.ds(0, ecount)],
                             e_send.at[t, e], e_recv.at[t, e], device(cx, cy)))
+                for k, p in enumerate(X_OUT[d]):
+                    xs[t, d, k] = values[p]
+            if place == 1:
+                wrap = jnp.where(gx == 0, 1, 0)
+                for far in (wrap, 1 - wrap):
+                    x_copies.append(remote(
+                        xs.at[t, far, pl.ds(0, count)], xr.at[t, far, pl.ds(0, count)],
+                        x_send.at[t, far], x_recv.at[t, far], device(1 - 2 * far, 0)))
         for d in (0, 1):
             y_copies.append(remote(
                 ys.at[t, d, pl.ds(0, count)], yr.at[t, d, pl.ds(0, count)],
@@ -266,9 +272,9 @@
         functools.partial(kernel, sizes),
         out_shape=jax.ShapeDtypeStruct(populations.shape, f32),
         in_specs=[
-            pl.BlockSpec(memory_space=pl.ANY),
-            pl.BlockSpec(memory_space=pl.ANY),
-            pl.BlockSpec(memory_space=pltpu.SMEM),
+            pl.BlockSpec(memory_space=pltpu.HBM),
+            pl.BlockSpec(memory_space=pltpu.HBM),
+            pl.BlockSpec(memory_space=pltpu.HBM),
         ],
         out_specs=pl.BlockSpec(memory_space=pltpu.VMEM),
         scratch_shapes=[
@@ -284,7 +290,8 @@
             vmem((STEPS, 4, 2) + line, f32),
             vmem((19, nx, ny, 128), f32),
             vmem((nx,) + block, jnp.int32),
-            dma((nx + 1,)),
+            pltpu.SMEM((19,), f32),
+            dma((nx + 2,)),
             dma((nx + 1,)),
             dma((nx + 1,)),
             dma((STEPS, 2)),

time: 28.5 us -> 25.3 us (0.89)
  Pallas kernels: 24.9 us -> 21.7 us
    pallas_call x1, Pallas kernels: 24.9 us -> 21.7 us  [shards(): pl.pallas_call(functools.partial(kernel, sizes), out_shape=jax.ShapeDtype...]
where the time goes in v2:
time: 25.3 us; the launch traced here: 25 us
  Pallas kernels  21.7 us (86%)
  local copies, waits for them, and re-layouts  3.32 us (13%)
    pallas_call x1, Pallas kernels, shards(): pl.pallas_call(functools.partial(kernel, sizes), out_shape=jax.ShapeDtype...  21.7 us
    unnamed x7, local copies, waits for them, and re-layouts  3.32 us

profile of v2, /device:TPU:0, one launch (start us, length us, event | category | flops | bytes accessed | tf_op | source)
XLA Modules:
  0.0 25.0 jit_solution(15287989211850211892)
XLA Ops:
  0.0 0.0 copy-start
  0.0 1.1 %copy-done = f32[19,4,16,128]{3,2,1,0:T(8,128)S(1)} copy-done((f32[19,4,16,128]{3,2,1,0:T(8,128)S(1)}, f32[19,4,16,128]{3,2,1,0:T(8,128)}, u32[]{:S(2)}) %copy-start) | copy-done | bytes 622616
  1.1 0.0 copy-start.1
  1.1 0.8 %copy-done.1 = s32[4,16,128]{2,1,0:T(8,128)S(1)} copy-done((s32[4,16,128]{2,1,0:T(8,128)S(1)}, s32[4,16,128]{2,1,0:T(8,128)}, u32[]{:S(2)}) %copy-start.1) | copy-done | bytes 32792
  1.8 0.0 copy-start.2
  1.8 0.7 %copy-done.2 = f32[19]{0:T(128)S(1)} copy-done((f32[19]{0:T(128)S(1)}, f32[19]{0:T(128)}, u32[]{:S(2)}) %copy-start.2) | copy-done | bytes 100
  2.5 21.7 %shard_map.37 = f32[19,4,16,128]{3,2,1,0:T(8,128)S(1)} custom-call(f32[19,4,16,128]{3,2,1,0:T(8,128)S(1)} %copy-done, s32[4,16,128]{2,1,0:T(8,128)S(1)} %copy-done.1, f32[19]{0:T(128)S(1)} %copy-done.2), custom_call_target="tpu_custom_call" | custom-call | tf_op jit(solution)/shard_map/pallas_call | solution.py:271
  24.2 0.8 %copy.5 = f32[19,4,16,128]{3,2,1,0:T(8,128)} copy(f32[19,4,16,128]{3,2,1,0:T(8,128)S(1)} %shard_map.37) | data formatting | bytes 1245184
Async XLA Ops:
  0.0 1.1 %copy-start = (f32[19,4,16,128]{3,2,1,0:T(8,128)S(1)}, f32[19,4,16,128]{3,2,1,0:T(8,128)}, u32[]{:S(2)}) copy-start(f32[19,4,16,128]{3,2,1,0:T(8,128)} %pop.1) | copy-start | bytes 1867780
  1.1 0.8 %copy-start.1 = (s32[4,16,128]{2,1,0:T(8,128)S(1)}, s32[4,16,128]{2,1,0:T(8,128)}, u32[]{:S(2)}) copy-start(s32[4,16,128]{2,1,0:T(8,128)} %sol.1) | copy-start | bytes 98308
  1.8 0.7 %copy-start.2 = (f32[19]{0:T(128)S(1)}, f32[19]{0:T(128)}, u32[]{:S(2)}) copy-start(f32[19]{0:T(128)} %rates_in.1) | copy-start | bytes 232

commit v3 on v2

--- a/solution.py
+++ b/solution.py
@@ -75,7 +75,8 @@
 
 
 def kernel(sizes, pop, sol, rates_in, out, held, relaxed, flag, blocked, xs, xr, ys, yr, es, er,
-           osend, iflag, rates, own_sem, in_send, in_recv, x_send, x_recv, y_send, y_recv, e_send, e_recv,
+           osend, iflag, rates, raw, iraw, fsend, xs0, ys0, es0, x0_send, x0_recv, y0_send, y0_recv,
+           e0_send, e0_recv, own_sem, in_send, in_recv, x_send, x_recv, y_send, y_recv, e_send, e_recv,
            o_send, o_recv):
     gxn, gyn, gzn, nx, ny = sizes
     pair = gzn == 2
@@ -93,11 +94,9 @@
     if pair:
         other = (gx, gy, 1 - gz)
         mine = pl.ds(pl.multiple_of(gz * ny, ny), ny)
-        others = pl.ds(pl.multiple_of((1 - gz) * ny, ny), ny)
         for x in order:
-            local.append(pltpu.make_async_copy(
-                pop.at[:, x, mine, :], held.at[:, x, gz], own_sem.at[x]))
-        local.append(pltpu.make_async_copy(sol.at[:, mine, :], iflag.at[:, gz], own_sem.at[nx]))
+            local.append(pltpu.make_async_copy(pop.at[:, x], raw.at[:, x], own_sem.at[x]))
+        local.append(pltpu.make_async_copy(sol, iraw, own_sem.at[nx]))
     else:
         for x in order:
             local.append(pltpu.make_async_copy(pop.at[:, x], held.at[:, x], own_sem.at[x]))
@@ -106,10 +105,18 @@
         copy.start()
 
     barrier = pltpu.get_barrier_semaphore()
-    around = [(dx, dy) for dx in (-1, 0, 1) for dy in (-1, 0, 1) if (dx, dy) != (0, 0)]
-    for dx, dy in around:
-        pl.semaphore_signal(barrier, inc=1, device_id=device(dx, dy), device_id_type=MESH)
-    pl.semaphore_wait(barrier, len(around))
+    near, ahead, back = lax.rem(gx + 1, gxn), lax.rem(gy + 1, gyn), lax.rem(gy + gyn - 1, gyn)
+    below = lax.rem(gx + gxn - 1, gxn)
+    if pair:
+        side = jnp.where(gz == 0, back, ahead)
+        around = [other] + [(i, gy, k) for i in (below, near) for k in (0, 1)]
+        around += [(i, side, k) for i in (below, gx, near) for k in (0, 1)]
+    else:
+        around = [device(dx, dy) for dx in (-1, 0, 1) for dy in (-1, 0, 1) if (dx, dy) != (0, 0)]
+    for to in around:
+        pl.semaphore_signal(barrier, inc=1, device_id=to, device_id_type=MESH)
+    if not pair:
+        pl.semaphore_wait(barrier, len(around))
 
     def remote(src, dst, send, recv, to):
         copy = pltpu.make_async_remote_copy(
@@ -119,13 +126,6 @@
         return copy
 
     moved = []
-    if pair:
-        for x in order:
-            moved.append(remote(pop.at[:, x, others, :], held.at[:, x, gz],
-                                in_send.at[x], in_recv.at[x], other))
-        moved.append(remote(sol.at[:, others, :], iflag.at[:, gz],
-                            in_send.at[nx], in_recv.at[nx], other))
-
     shape = (gzn, ny, 128)
     row = lax.broadcasted_iota(jnp.int32, shape, 1)
     lane = lax.broadcasted_iota(jnp.int32, shape, 2)
@@ -135,8 +135,6 @@
 
     def arrived(index):
         local[index].wait()
-        if pair:
-            moved[index].wait_recv()
 
     def shifted(plane, halo, velocity):
         cx, cy, cz = velocity
@@ -171,9 +169,119 @@
 
         return shifted(plane, halo, (cx, cy, cz))
 
+    def first_step():
+        lower = gz == 0
+        local[nx].wait()
+        flags = [iraw[x].astype(jnp.float32) for x in range(nx)]
+        part = lambda value, h: value[h * ny : (h + 1) * ny]
+        line = lambda value, at: value[at : at + 1]
+        feed = {(0, 1): ny - 1, (0, 0): 2 * ny - 1, (1, 0): ny, (1, 1): 0}
+
+        def put_y(k, x, d, value):
+            ys0[0, d, k, x] = line(value, feed[d, d])
+            ys0[1, d, k, x] = line(value, feed[d, 1 - d])
+
+        for x in range(nx):
+            flag[x, gz] = jnp.where(lower, part(flags[x], 0), part(flags[x], 1))
+            fsend[x] = jnp.where(lower, part(flags[x], 1), part(flags[x], 0))
+            for d in (0, 1):
+                put_y(5, x, d, flags[x])
+        for h in (0, 1):
+            xs0[h, 0, 5] = part(flags[nx - 1], h)
+            xs0[h, 1, 5] = part(flags[0], h)
+            for e, p in enumerate(EDGE):
+                cx, cy, _ = VELOCITY[p]
+                es0[h, e, 1] = line(flags[nx - 1 if cx > 0 else 0], feed[0 if cy > 0 else 1, h])
+
+        def one(place, x):
+            arrived(place)
+            values = collide([raw[index, x] for index in range(19)], rate)
+            for index in range(19):
+                low, high = part(values[index], 0), part(values[index], 1)
+                relaxed[index, x, gz] = jnp.where(lower, low, high)
+                osend[index, x] = jnp.where(lower, high, low)
+            for d in (0, 1):
+                for k, p in enumerate(Y_OUT[d]):
+                    put_y(k, x, d, values[p])
+            return values
+
+        faces = {x: one(place, x) for place, x in enumerate(order[:2])}
+        for h in (0, 1):
+            for e, p in enumerate(EDGE):
+                cx, cy, _ = VELOCITY[p]
+                es0[h, e, 0] = line(faces[nx - 1 if cx > 0 else 0][p], feed[0 if cy > 0 else 1, h])
+            for k in range(5):
+                xs0[h, 0, k] = part(faces[nx - 1][X_OUT[0][k]], h)
+                xs0[h, 1, k] = part(faces[0][X_OUT[1][k]], h)
+        pl.semaphore_wait(barrier, len(around))
+        e_copies, x_copies, y_copies, r_copies = [], [], [], []
+        for h in (0, 1):
+            for e, p in enumerate(EDGE):
+                cx, cy, _ = VELOCITY[p]
+                to_y = gy if (cy > 0) == (h == 1) else (ahead if cy > 0 else back)
+                e_copies.append(remote(es0.at[h, e], er.at[0, e, :, gz], e0_send.at[h, e],
+                                       e0_recv.at[gz, e], (near if cx > 0 else below, to_y, h)))
+        wrap = jnp.where(gx == 0, 1, 0)
+        for far in (wrap, 1 - wrap):
+            for h in (0, 1):
+                x_copies.append(remote(
+                    xs0.at[h, far], xr.at[0, far, :, gz], x0_send.at[h, far],
+                    x0_recv.at[gz, far], (jnp.where(far == 0, near, below), gy, h)))
+        for place, x in enumerate(order[2:]):
+            one(place + 2, x)
+        for d, to in ((0, (gx, ahead, 0)), (1, (gx, back, 1))):
+            y_copies.append(remote(ys0.at[0, d], yr.at[0, d, :, :, gz], y0_send.at[d],
+                                   y0_recv.at[gz], to))
+        y_copies.append(remote(ys0.at[1, gz], yr.at[0, gz, :, :, gz], y0_send.at[2],
+                               y0_recv.at[2], other))
+        yr[0, 1 - gz, :, :, gz] = ys0[1, 1 - gz]
+        r_copies.append(remote(fsend, flag.at[:, gz], in_send.at[nx], in_recv.at[nx], other))
+        for x in order:
+            r_copies.append(remote(osend.at[:, x], relaxed.at[:, x, gz], in_send.at[x],
+                                   in_recv.at[x], other))
+
+        def faces_in():
+            for d in (0, 1):
+                for k in (0, 1):
+                    pltpu.make_async_remote_copy(
+                        src_ref=xs0.at[k, d], dst_ref=xr.at[0, d, :, k], send_sem=x0_send.at[k, d],
+                        recv_sem=x0_recv.at[k, d], device_id=other,
+                        device_id_type=MESH).wait_recv()
+            for e in range(4):
+                for k in (0, 1):
+                    pltpu.make_async_remote_copy(
+                        src_ref=es0.at[k, e], dst_ref=er.at[0, e, :, k], send_sem=e0_send.at[k, e],
+                        recv_sem=e0_recv.at[k, e], device_id=other,
+                        device_id_type=MESH).wait_recv()
+
+        def rows_in():
+            for k in (0, 1):
+                pltpu.make_async_remote_copy(
+                    src_ref=ys0.at[0, 0], dst_ref=yr.at[0, gz, :, :, k], send_sem=y0_send.at[0],
+                    recv_sem=y0_recv.at[k], device_id=other, device_id_type=MESH).wait_recv()
+            pltpu.make_async_remote_copy(
+                src_ref=ys0.at[1, gz], dst_ref=yr.at[0, 1 - gz, :, :, 1 - gz],
+                send_sem=y0_send.at[2], recv_sem=y0_recv.at[2], device_id=other,
+                device_id_type=MESH).wait_recv()
+            for place, x in enumerate([nx] + order):
+                pltpu.make_async_remote_copy(
+                    src_ref=fsend if place == 0 else osend.at[:, x],
+                    dst_ref=flag.at[:, 1 - gz] if place == 0 else relaxed.at[:, x, 1 - gz],
+                    send_sem=in_send.at[x], recv_sem=in_recv.at[x], device_id=other,
+                    device_id_type=MESH).wait_recv()
+
+        for copy in r_copies:
+            first_sends.append(copy)
+        sent.extend(e_copies + x_copies + y_copies)
+        return rows_in, faces_in
+
+    first_sends = []
+    rows_in = faces_in = None
+    if pair:
+        rows_in, faces_in = first_step()
     for t in range(STEPS):
         last = t == STEPS - 1
-        if t == 0:
+        if t == 0 and not pair:
             arrived(nx)
             for x in range(nx):
                 flag[x] = iflag[x].astype(jnp.float32)
@@ -188,7 +296,7 @@
         count = 6 if t == 0 else 5
         ecount = 2 if t == 0 else 1
         x_copies, e_copies, y_copies = [], [], []
-        for place, x in enumerate(order):
+        for place, x in enumerate(order if t or not pair else []):
             if t == 0:
                 arrived(place)
             values = collide([held[index, x] for index in range(19)], rate)
@@ -215,17 +323,24 @@
                     x_copies.append(remote(
                         xs.at[t, far, pl.ds(0, count)], xr.at[t, far, pl.ds(0, count)],
                         x_send.at[t, far], x_recv.at[t, far], device(1 - 2 * far, 0)))
-        for d in (0, 1):
+        for d in (0, 1) if t or not pair else ():
             y_copies.append(remote(
                 ys.at[t, d, pl.ds(0, count)], yr.at[t, d, pl.ds(0, count)],
                 y_send.at[t, d], y_recv.at[t, d], device(0, 1 if d == 0 else -1)))
         sent += x_copies + e_copies + y_copies
         for copy in y_copies:
             copy.wait_recv()
+        if t == 0 and pair:
+            rows_in()
         for place, x in enumerate(order[2:] + order[:2]):
             if place == nx - 2:
                 for copy in x_copies + e_copies:
                     copy.wait_recv()
+                if t == 0 and pair:
+                    faces_in()
+            if last and place == 0:
+                for copy in first_sends:
+                    copy.wait_send()
             rock = flag[x] > 0.5
             for p in range(19):
                 if p == 0:
@@ -252,7 +367,7 @@
                 sent.append(copy)
                 moved.append(copy)
     if pair:
-        for copy in moved[nx + 1:]:
+        for copy in moved:
             copy.wait_recv()
     for copy in sent:
         copy.wait_send()
@@ -291,6 +406,18 @@
             vmem((19, nx, ny, 128), f32),
             vmem((nx,) + block, jnp.int32),
             pltpu.SMEM((19,), f32),
+            vmem((19, nx, gzn * ny, 128), f32),
+            vmem((nx, gzn * ny, 128), jnp.int32),
+            vmem((nx, ny, 128), f32),
+            vmem((2, 2, 6, ny, 128), f32),
+            vmem((2, 2, 6, nx, 1, 128), f32),
+            vmem((2, 4, 2, 1, 128), f32),
+            dma((2, 2)),
+            dma((2, 2)),
+            dma((3,)),
+            dma((3,)),
+            dma((2, 4)),
+            dma((2, 4)),
             dma((nx + 2,)),
             dma((nx + 1,)),
             dma((nx + 1,)),

time: 25.3 us -> 24.4 us (0.964)
  Pallas kernels: 21.7 us -> 20.9 us
    pallas_call x1, Pallas kernels: 21.7 us -> 20.9 us  [shards(): pl.pallas_call(functools.partial(kernel, sizes), out_shape=jax.ShapeDtype...]
where the time goes in v3:
time: 24.4 us; the launch traced here: 24.2 us
  Pallas kernels  20.9 us (86%)
  local copies, waits for them, and re-layouts  3.32 us (14%)
    pallas_call x1, Pallas kernels, shards(): pl.pallas_call(functools.partial(kernel, sizes), out_shape=jax.ShapeDtype...  20.9 us
    unnamed x7, local copies, waits for them, and re-layouts  3.32 us

profile of v3, /device:TPU:0, one launch (start us, length us, event | category | flops | bytes accessed | tf_op | source)
XLA Modules:
  0.0 24.2 jit_solution(12753968818446192780)
XLA Ops:
  0.0 0.0 copy-start
  0.0 1.1 %copy-done = f32[19,4,16,128]{3,2,1,0:T(8,128)S(1)} copy-done((f32[19,4,16,128]{3,2,1,0:T(8,128)S(1)}, f32[19,4,16,128]{3,2,1,0:T(8,128)}, u32[]{:S(2)}) %copy-start) | copy-done | bytes 622616
  1.1 0.0 copy-start.1
  1.1 0.8 %copy-done.1 = s32[4,16,128]{2,1,0:T(8,128)S(1)} copy-done((s32[4,16,128]{2,1,0:T(8,128)S(1)}, s32[4,16,128]{2,1,0:T(8,128)}, u32[]{:S(2)}) %copy-start.1) | copy-done | bytes 32792
  1.8 0.0 copy-start.2
  1.8 0.7 %copy-done.2 = f32[19]{0:T(128)S(1)} copy-done((f32[19]{0:T(128)S(1)}, f32[19]{0:T(128)}, u32[]{:S(2)}) %copy-start.2) | copy-done | bytes 100
  2.5 20.9 %shard_map.37 = f32[19,4,16,128]{3,2,1,0:T(8,128)S(1)} custom-call(f32[19,4,16,128]{3,2,1,0:T(8,128)S(1)} %copy-done, s32[4,16,128]{2,1,0:T(8,128)S(1)} %copy-done.1, f32[19]{0:T(128)S(1)} %copy-done.2), custom_call_target="tpu_custom_call" | custom-call | tf_op jit(solution)/shard_map/pallas_call | solution.py:386
  23.4 0.8 %copy.5 = f32[19,4,16,128]{3,2,1,0:T(8,128)} copy(f32[19,4,16,128]{3,2,1,0:T(8,128)S(1)} %shard_map.37) | data formatting | bytes 1245184
Async XLA Ops:
  0.0 1.1 %copy-start = (f32[19,4,16,128]{3,2,1,0:T(8,128)S(1)}, f32[19,4,16,128]{3,2,1,0:T(8,128)}, u32[]{:S(2)}) copy-start(f32[19,4,16,128]{3,2,1,0:T(8,128)} %pop.1) | copy-start | bytes 1867780
  1.1 0.8 %copy-start.1 = (s32[4,16,128]{2,1,0:T(8,128)S(1)}, s32[4,16,128]{2,1,0:T(8,128)}, u32[]{:S(2)}) copy-start(s32[4,16,128]{2,1,0:T(8,128)} %sol.1) | copy-start | bytes 98308
  1.8 0.7 %copy-start.2 = (f32[19]{0:T(128)S(1)}, f32[19]{0:T(128)}, u32[]{:S(2)}) copy-start(f32[19]{0:T(128)} %rates_in.1) | copy-start | bytes 232

commit v4 on v3

--- a/solution.py
+++ b/solution.py
@@ -101,20 +101,20 @@
         for x in order:
             local.append(pltpu.make_async_copy(pop.at[:, x], held.at[:, x], own_sem.at[x]))
         local.append(pltpu.make_async_copy(sol, iflag, own_sem.at[nx]))
-    for copy in local:
-        copy.start()
 
     barrier = pltpu.get_barrier_semaphore()
     near, ahead, back = lax.rem(gx + 1, gxn), lax.rem(gy + 1, gyn), lax.rem(gy + gyn - 1, gyn)
     below = lax.rem(gx + gxn - 1, gxn)
     if pair:
         side = jnp.where(gz == 0, back, ahead)
-        around = [other] + [(i, gy, k) for i in (below, near) for k in (0, 1)]
-        around += [(i, side, k) for i in (below, gx, near) for k in (0, 1)]
+        around = [(i, side, k) for i in (below, near, gx) for k in (0, 1)]
+        around += [(i, gy, k) for i in (below, near) for k in (0, 1)] + [other]
     else:
         around = [device(dx, dy) for dx in (-1, 0, 1) for dy in (-1, 0, 1) if (dx, dy) != (0, 0)]
     for to in around:
         pl.semaphore_signal(barrier, inc=1, device_id=to, device_id_type=MESH)
+    for copy in local:
+        copy.start()
     if not pair:
         pl.semaphore_wait(barrier, len(around))
 
@@ -132,6 +132,7 @@
     rates_copy.wait()
     rate = [rates[index] for index in range(19)]
     sent = list(moved)
+    leaving = []
 
     def arrived(index):
         local[index].wait()
@@ -327,20 +328,25 @@
             y_copies.append(remote(
                 ys.at[t, d, pl.ds(0, count)], yr.at[t, d, pl.ds(0, count)],
                 y_send.at[t, d], y_recv.at[t, d], device(0, 1 if d == 0 else -1)))
+        while sent:
+            sent.pop().wait_send()
         sent += x_copies + e_copies + y_copies
+        if last:
+            while first_sends:
+                first_sends.pop().wait_send()
         for copy in y_copies:
             copy.wait_recv()
         if t == 0 and pair:
             rows_in()
         for place, x in enumerate(order[2:] + order[:2]):
             if place == nx - 2:
+                if last:
+                    while sent and len(sent) > len(leaving):
+                        sent.pop(0).wait_send()
                 for copy in x_copies + e_copies:
                     copy.wait_recv()
                 if t == 0 and pair:
                     faces_in()
-            if last and place == 0:
-                for copy in first_sends:
-                    copy.wait_send()
             rock = flag[x] > 0.5
             for p in range(19):
                 if p == 0:
@@ -365,6 +371,7 @@
                 copy = remote(osend.at[:, x], out.at[:, x, mine, :],
                               o_send.at[x], o_recv.at[x], other)
                 sent.append(copy)
+                leaving.append(copy)
                 moved.append(copy)
     if pair:
         for copy in moved:

time: 24.4 us -> 24.2 us (level)
  Pallas kernels: 20.9 us -> 20.6 us
    pallas_call x1, Pallas kernels: 20.9 us -> 20.6 us  [shards(): pl.pallas_call(functools.partial(kernel, sizes), out_shape=jax.ShapeDtype...]
where the time goes in v4:
time: 24.2 us; the launch traced here: 24 us
  Pallas kernels  20.6 us (85%)
  local copies, waits for them, and re-layouts  3.32 us (14%)
    pallas_call x1, Pallas kernels, shards(): pl.pallas_call(functools.partial(kernel, sizes), out_shape=jax.ShapeDtype...  20.6 us
    unnamed x7, local copies, waits for them, and re-layouts  3.32 us

profile of v4, /device:TPU:0, one launch (start us, length us, event | category | flops | bytes accessed | tf_op | source)
XLA Modules:
  0.0 24.0 jit_solution(15436831292171639803)
XLA Ops:
  0.0 0.0 copy-start
  0.0 1.1 %copy-done = f32[19,4,16,128]{3,2,1,0:T(8,128)S(1)} copy-done((f32[19,4,16,128]{3,2,1,0:T(8,128)S(1)}, f32[19,4,16,128]{3,2,1,0:T(8,128)}, u32[]{:S(2)}) %copy-start) | copy-done | bytes 622616
  1.1 0.0 copy-start.1
  1.1 0.8 %copy-done.1 = s32[4,16,128]{2,1,0:T(8,128)S(1)} copy-done((s32[4,16,128]{2,1,0:T(8,128)S(1)}, s32[4,16,128]{2,1,0:T(8,128)}, u32[]{:S(2)}) %copy-start.1) | copy-done | bytes 32792
  1.8 0.0 copy-start.2
  1.8 0.7 %copy-done.2 = f32[19]{0:T(128)S(1)} copy-done((f32[19]{0:T(128)S(1)}, f32[19]{0:T(128)}, u32[]{:S(2)}) %copy-start.2) | copy-done | bytes 100
  2.5 20.6 %shard_map.37 = f32[19,4,16,128]{3,2,1,0:T(8,128)S(1)} custom-call(f32[19,4,16,128]{3,2,1,0:T(8,128)S(1)} %copy-done, s32[4,16,128]{2,1,0:T(8,128)S(1)} %copy-done.1, f32[19]{0:T(128)S(1)} %copy-done.2), custom_call_target="tpu_custom_call" | custom-call | tf_op jit(solution)/shard_map/pallas_call | solution.py:393
  23.1 0.8 %copy.5 = f32[19,4,16,128]{3,2,1,0:T(8,128)} copy(f32[19,4,16,128]{3,2,1,0:T(8,128)S(1)} %shard_map.37) | data formatting | bytes 1245184
Async XLA Ops:
  0.0 1.1 %copy-start = (f32[19,4,16,128]{3,2,1,0:T(8,128)S(1)}, f32[19,4,16,128]{3,2,1,0:T(8,128)}, u32[]{:S(2)}) copy-start(f32[19,4,16,128]{3,2,1,0:T(8,128)} %pop.1) | copy-start | bytes 1867780
  1.1 0.8 %copy-start.1 = (s32[4,16,128]{2,1,0:T(8,128)S(1)}, s32[4,16,128]{2,1,0:T(8,128)}, u32[]{:S(2)}) copy-start(s32[4,16,128]{2,1,0:T(8,128)} %sol.1) | copy-start | bytes 98308
  1.8 0.7 %copy-start.2 = (f32[19]{0:T(128)S(1)}, f32[19]{0:T(128)}, u32[]{:S(2)}) copy-start(f32[19]{0:T(128)} %rates_in.1) | copy-start | bytes 232

commit v5 on v4

--- a/solution.py
+++ b/solution.py
@@ -214,6 +214,8 @@
             for k in range(5):
                 xs0[h, 0, k] = part(faces[nx - 1][X_OUT[0][k]], h)
                 xs0[h, 1, k] = part(faces[0][X_OUT[1][k]], h)
+        for place, x in enumerate(order[2:]):
+            one(place + 2, x)
         pl.semaphore_wait(barrier, len(around))
         e_copies, x_copies, y_copies, r_copies = [], [], [], []
         for h in (0, 1):
@@ -228,8 +230,6 @@
                 x_copies.append(remote(
                     xs0.at[h, far], xr.at[0, far, :, gz], x0_send.at[h, far],
                     x0_recv.at[gz, far], (jnp.where(far == 0, near, below), gy, h)))
-        for place, x in enumerate(order[2:]):
-            one(place + 2, x)
         for d, to in ((0, (gx, ahead, 0)), (1, (gx, back, 1))):
             y_copies.append(remote(ys0.at[0, d], yr.at[0, d, :, :, gz], y0_send.at[d],
                                    y0_recv.at[gz], to))
@@ -237,9 +237,7 @@
                                y0_recv.at[2], other))
         yr[0, 1 - gz, :, :, gz] = ys0[1, 1 - gz]
         r_copies.append(remote(fsend, flag.at[:, gz], in_send.at[nx], in_recv.at[nx], other))
-        for x in order:
-            r_copies.append(remote(osend.at[:, x], relaxed.at[:, x, gz], in_send.at[x],
-                                   in_recv.at[x], other))
+        r_copies.append(remote(osend, relaxed.at[:, :, gz], in_send.at[0], in_recv.at[0], other))
 
         def faces_in():
             for d in (0, 1):
@@ -264,10 +262,10 @@
                 src_ref=ys0.at[1, gz], dst_ref=yr.at[0, 1 - gz, :, :, 1 - gz],
                 send_sem=y0_send.at[2], recv_sem=y0_recv.at[2], device_id=other,
                 device_id_type=MESH).wait_recv()
-            for place, x in enumerate([nx] + order):
+            for place, x in enumerate([nx, 0]):
                 pltpu.make_async_remote_copy(
-                    src_ref=fsend if place == 0 else osend.at[:, x],
-                    dst_ref=flag.at[:, 1 - gz] if place == 0 else relaxed.at[:, x, 1 - gz],
+                    src_ref=fsend if place == 0 else osend,
+                    dst_ref=flag.at[:, 1 - gz] if place == 0 else relaxed.at[:, :, 1 - gz],
                     send_sem=in_send.at[x], recv_sem=in_recv.at[x], device_id=other,
                     device_id_type=MESH).wait_recv()
 

time: 24.2 us -> 24.2 us (level)
  no operation moved by 1% of the time
where the time goes in v5:
time: 24.2 us; the launch traced here: 24 us
  Pallas kernels  20.6 us (85%)
  local copies, waits for them, and re-layouts  3.32 us (14%)
    pallas_call x1, Pallas kernels, shards(): pl.pallas_call(functools.partial(kernel, sizes), out_shape=jax.ShapeDtype...  20.6 us
    unnamed x7, local copies, waits for them, and re-layouts  3.32 us

profile of v5, /device:TPU:0, one launch (start us, length us, event | category | flops | bytes accessed | tf_op | source)
XLA Modules:
  0.0 24.0 jit_solution(9626420495028569099)
XLA Ops:
  0.0 0.0 copy-start
  0.0 1.1 %copy-done = f32[19,4,16,128]{3,2,1,0:T(8,128)S(1)} copy-done((f32[19,4,16,128]{3,2,1,0:T(8,128)S(1)}, f32[19,4,16,128]{3,2,1,0:T(8,128)}, u32[]{:S(2)}) %copy-start) | copy-done | bytes 622616
  1.1 0.0 copy-start.1
  1.1 0.8 %copy-done.1 = s32[4,16,128]{2,1,0:T(8,128)S(1)} copy-done((s32[4,16,128]{2,1,0:T(8,128)S(1)}, s32[4,16,128]{2,1,0:T(8,128)}, u32[]{:S(2)}) %copy-start.1) | copy-done | bytes 32792
  1.8 0.0 copy-start.2
  1.8 0.7 %copy-done.2 = f32[19]{0:T(128)S(1)} copy-done((f32[19]{0:T(128)S(1)}, f32[19]{0:T(128)}, u32[]{:S(2)}) %copy-start.2) | copy-done | bytes 100
  2.5 20.6 %shard_map.37 = f32[19,4,16,128]{3,2,1,0:T(8,128)S(1)} custom-call(f32[19,4,16,128]{3,2,1,0:T(8,128)S(1)} %copy-done, s32[4,16,128]{2,1,0:T(8,128)S(1)} %copy-done.1, f32[19]{0:T(128)S(1)} %copy-done.2), custom_call_target="tpu_custom_call" | custom-call | tf_op jit(solution)/shard_map/pallas_call | solution.py:391
  23.1 0.8 %copy.5 = f32[19,4,16,128]{3,2,1,0:T(8,128)} copy(f32[19,4,16,128]{3,2,1,0:T(8,128)S(1)} %shard_map.37) | data formatting | bytes 1245184
Async XLA Ops:
  0.0 1.1 %copy-start = (f32[19,4,16,128]{3,2,1,0:T(8,128)S(1)}, f32[19,4,16,128]{3,2,1,0:T(8,128)}, u32[]{:S(2)}) copy-start(f32[19,4,16,128]{3,2,1,0:T(8,128)} %pop.1) | copy-start | bytes 1867780
  1.1 0.8 %copy-start.1 = (s32[4,16,128]{2,1,0:T(8,128)S(1)}, s32[4,16,128]{2,1,0:T(8,128)}, u32[]{:S(2)}) copy-start(s32[4,16,128]{2,1,0:T(8,128)} %sol.1) | copy-start | bytes 98308
  1.8 0.7 %copy-start.2 = (f32[19]{0:T(128)S(1)}, f32[19]{0:T(128)}, u32[]{:S(2)}) copy-start(f32[19]{0:T(128)} %rates_in.1) | copy-start | bytes 232
